TPU v7x, 32 devices: a whole 2x2x4 slice. The times are simulated.
32 devices in a mesh: vir: 8 (over y, x, core), out: 4 (over z).
Axes of the slice: x: 2, y: 2, z: 4, core: 2. Of those that a mesh axis runs over, the one named last changes fastest.
Arguments:
- factors: bfloat16 [512, 512, 1536], P('out', 'vir'), may hold values from -2.5 to 2.5
- amplitudes: bfloat16 [128, 512, 512], P('out', 'vir'), may hold values from -0.015991211 to 0.015991211
Outputs:
- ladder: float32 [2, 128, 512], P(None, 'vir', 'out')
All inputs are finite; a program needn't handle non-finite values.
Results may differ from a plain program's by a relative error of at most 0.0029.
Values may be sent and summed in bfloat16 or wider, within the bound.
No kernel may reach another device: no remote copies, remote signals or barrier semaphores. Data moves between devices by JAX's collectives and lax.ppermute only.
A program may use at most 128 MiB of HBM per device.

v0:
```python
import jax
import jax.numpy as jnp
from jax import lax
from jax.sharding import PartitionSpec as P

BB = 2


def spread(block, axis, source):
    block = jnp.where(lax.axis_index(axis) == source, block, jnp.zeros_like(block))
    return lax.psum(block, axis)


def body(factors, amplitudes):
    a_rows, c_rows, aux_len = factors.shape
    local_rows = factors.reshape(a_rows * c_rows, aux_len)
    every_pair = lax.all_gather(amplitudes, "out", axis=0, tiled=True)
    batch_rows = factors[:BB]
    shared = spread(batch_rows, "out", 0)
    gathered = lax.all_gather(shared, "vir", axis=1, tiled=True)
    piece_len = gathered.shape[1]
    tiles = lax.dot_general(
        local_rows, gathered, (((1,), (2,)), ((), ())), preferred_element_type=jnp.float32
    )
    integral = tiles.astype(jnp.bfloat16).reshape(a_rows, c_rows, BB, piece_len)
    terms = jnp.einsum("acbd,pcd->bpa", integral, every_pair, preferred_element_type=jnp.float32)
    return lax.psum_scatter(terms, "vir", scatter_dimension=1, tiled=True)


def solution(mesh):
    placed = (P("out", "vir", None), P("out", "vir", None))
    return jax.shard_map(
        body, mesh=mesh, in_specs=placed, out_specs=P(None, "vir", "out"), check_vma=False
    )
```

profile of v0, /device:TPU:16, one launch (start us, length us, event | category | flops | bytes accessed | tf_op | source)
XLA Modules:
  0.0 324.3 jit_solution(10722758401791957893)
XLA Ops:
  6.5 0.0 all-reduce.4.cloned.1.call-start
  6.5 1.8 slice_select_fusion
  8.3 0.0 all-reduce.4.cloned.1.call-update
  8.3 0.0 all-gather.3.cloned.1.call-start
  8.4 39.0 %all-reduce.4.cloned.1.call-done = bf16[2,64,1536]{2,1,0:T(8,128)(2,1)} async-done(((bf16[2,64,1536]{2,1,0:T(8,128)(2,1)}), bf16[2,64,1536]{2,1,0:T(8,128)(2,1)}) %all-reduce.4.cloned.1.call-update) | async-done | bytes 393232 | tf_op jit(solution)/shard_map/psum | solution.py:11
  47.3 0.0 all-gather.3.cloned.1.call-update
  47.4 0.0 all-gather.5.cloned.1.call-start
  47.4 4.1 %copy.11 = bf16[32,64,512]{2,0,1:T(8,128)(2,1)} copy(bf16[32,64,512]{2,1,0:T(8,128)(2,1)} %param.3) | data formatting | bytes 4194304 | tf_op args[1]
  51.5 0.0 all-gather.5.cloned.1.call-update
  51.5 0.0 all-reduce.6.cloned.1.call-start
  51.6 30.3 %all-gather.3.cloned.1.call-done = bf16[2,512,1536]{2,1,0:T(8,128)(2,1)} async-done(((bf16[2,64,1536]{2,1,0:T(8,128)(2,1)}), bf16[2,512,1536]{2,1,0:T(8,128)(2,1)}) %all-gather.3.cloned.1.call-update) | async-done | bytes 3145744 | tf_op jit(solution)/shard_map/all_gather | solution.py:20
  81.9 32.4 %convert_bitcast_fusion = bf16[8192,2,512]{0,2,1:T(8,128)(2,1)} fusion(bf16[2,512,1536]{2,1,0:T(8,128)(2,1)} %all-gather.3.cloned.1.call-done, bf16[8192,1536,1]{1,0,2:T(8,128)(2,1)} %bitcast.20), kind=kOutput, calls=%fused_computation.2 | convolution fusion | flops 25778192384 | bytes 45088768 | tf_op jit(solution)/shard_map/dot_general | solution.py:22
  114.4 21.3 %copy.10 = bf16[8192,2,512]{2,0,1:T(8,128)(2,1)} copy(bf16[8192,2,512]{0,2,1:T(8,128)(2,1)} %convert_bitcast_fusion) | data formatting | bytes 33554432 | tf_op jit(solution)/shard_map/convert_element_type | solution.py:25
  135.6 0.0 copy-start
  135.6 95.8 %all-gather.5.cloned.1.call-done = bf16[128,64,512]{2,0,1:T(8,128)(2,1)} async-done(((bf16[32,64,512]{2,0,1:T(8,128)(2,1)}), bf16[128,64,512]{2,0,1:T(8,128)(2,1)}) %all-gather.5.cloned.1.call-update) | async-done | bytes 8388624 | tf_op jit(solution)/shard_map/all_gather | solution.py:17
  231.5 31.1 %fusion.3 = f32[2,128,128]{1,2,0:T(8,128)S(1)} fusion(bf16[128,64,512]{2,0,1:T(8,128)(2,1)} %all-gather.5.cloned.1.call-done, bf16[128,64,2,512]{3,1,0,2:T(8,128)(2,1)} %bitcast.19), kind=kOutput, calls=%fused_computation.4 | convolution fusion | flops 2147483648 | bytes 25296896 | tf_op jit(solution)/shard_map/acbd,pcd->bpa/dot_general | solution.py:26
  262.5 0.8 copy.13
  263.3 0.0 all-reduce.6.cloned.1.call-update
  263.3 0.0 copy-done
  263.3 0.6 dynamic-slice
  264.6 51.8 %all-reduce.6.cloned.1.call-done = f32[2,128,128]{2,0,1:T(2,128)} async-done(((f32[2,128,128]{2,0,1:T(2,128)}), f32[2,128,128]{2,0,1:T(2,128)}) %all-reduce.6.cloned.1.call-update) | async-done | bytes 131088
  316.4 0.7 constant_dynamic-slice_fusion
  317.1 0.6 copy.14
Async XLA Ops:
  6.5 40.8 %all-reduce.4.cloned.1.call-start = ((), (), s32[]{:S(2)}) async-start(), calls=%async_computation | async-start | bytes 786432 | tf_op jit(solution)/shard_map/psum | solution.py:11
  8.3 73.6 %all-gather.3.cloned.1.call-start = ((), (), s32[]{:S(2)}) async-start(), calls=%async_computation.1 | async-start | bytes 3538944 | tf_op jit(solution)/shard_map/all_gather | solution.py:20
  47.4 184.1 %all-gather.5.cloned.1.call-start = ((), (), s32[]{:S(2)}) async-start(), calls=%async_computation.2 | async-start | bytes 10485760 | tf_op jit(solution)/shard_map/all_gather | solution.py:17
  51.5 264.9 %all-reduce.6.cloned.1.call-start = ((), (), s32[]{:S(2)}) async-start(), calls=%async_computation.3 | async-start | bytes 262144
  135.6 127.7 %copy-start = (u32[32]{0:T(128)S(1)}, u32[32]{0:T(128)}, u32[]{:S(2)}) copy-start(u32[32]{0:T(128)} %constant.10) | copy-start | bytes 388
Sparse Core Ops, SparseCore 0:
  9.7 37.5 all-reduce.3
  49.4 32.4 all-gather.2
  83.6 147.8 all-gather.4
  263.5 52.8 all-reduce.5
where the time goes:
time: 327 us; the launch traced here: 324 us
  waiting for transfers between devices  217 us (66%)
  matrix products  63.5 us (19%)
  local copies, waits for them, and re-layouts  28 us (9%)
  between operations  13.8 us (4%)
    all_gather x1, waiting for transfers between devices, body(): every_pair = lax.all_gather(amplitudes, 'out', axis=0, tiled=True)  95.8 us
    unnamed x5, waiting for transfers between devices  51.9 us
    psum x1, waiting for transfers between devices, spread(): return lax.psum(block, axis)  39 us
    dot_general x1, matrix products, body(): lax.dot_general(local_rows, gathered, (((1,), (2,)), ((), ())), preferred...  32.4 us
    dot_general x1, matrix products, body(): jnp.einsum('acbd,pcd->bpa', integral, every_pair, preferred_element_type=...  31.1 us
    all_gather x1, waiting for transfers between devices, body(): gathered = lax.all_gather(shared, 'vir', axis=1, tiled=True)  30.3 us
    convert_element_type x1, local copies, waits for them, and re-layouts, body(): integral = tiles.astype(jnp.bfloat16).reshape(a_rows, c_rows, BB, piece_len)  21.3 us
  transfers between devices with their start and end apart: 4, of which 4 were waited for; matrix products, arithmetic and copies ran while one was open for 18% of the time, Pallas kernels for 0%

commit v1 on v0

v1 whole, which is shorter than its diff:
```python
import functools

import jax
import jax.numpy as jnp
from jax import lax
from jax.experimental import pallas as pl
from jax.experimental.pallas import tpu as pltpu
from jax.sharding import PartitionSpec as P

BB = 2
LANES = 128
NT = (((1,), (1,)), ((), ()))


def largest_part(extent, limit):
    part = min(extent, limit)
    while extent % part:
        part -= 1
    return part


def integral_kernel(factor_ref, batch_ref, out_ref, tile_ref):
    a_len, c_len, aux_len = factor_ref.shape
    d_len = out_ref.shape[3]
    rows = factor_ref[...].reshape(a_len * c_len, aux_len)
    for b in range(out_ref.shape[1]):
        tile = lax.dot_general(rows, batch_ref[b], NT, preferred_element_type=jnp.float32)
        for j in range(d_len // LANES):
            tile_ref[j] = tile[:, j * LANES : (j + 1) * LANES]
        for c in range(c_len):
            for j in range(d_len // LANES):
                picked = tile_ref[j, pl.ds(c, a_len, stride=c_len), :]
                out_ref[c, b, :, j * LANES : (j + 1) * LANES] = picked.astype(jnp.bfloat16)


def integrals(factors, batch):
    a_rows, c_rows, aux_len = factors.shape
    bb, d_len, _ = batch.shape
    a_len = largest_part(a_rows, 16)
    return pl.pallas_call(
        integral_kernel,
        grid=(a_rows // a_len,),
        in_specs=[
            pl.BlockSpec((a_len, c_rows, aux_len), lambda i: (i, 0, 0)),
            pl.BlockSpec((bb, d_len, aux_len), lambda i: (0, 0, 0)),
        ],
        out_specs=pl.BlockSpec((c_rows, bb, a_len, d_len), lambda i: (0, 0, i, 0)),
        out_shape=jax.ShapeDtypeStruct((c_rows, bb, a_rows, d_len), jnp.bfloat16),
        scratch_shapes=[pltpu.VMEM((d_len // LANES, a_len * c_rows, LANES), jnp.float32)],
        compiler_params=pltpu.CompilerParams(vmem_limit_bytes=48 * 2**20),
        cost_estimate=pl.CostEstimate(
            flops=2 * a_rows * c_rows * bb * d_len * aux_len,
            bytes_accessed=2 * (factors.size + batch.size + a_rows * c_rows * bb * d_len),
            transcendentals=0,
        ),
    )(factors, batch)


def ladder_kernel(count, *refs):
    tau_refs, integral_ref, out_ref = refs[:count], refs[count], refs[count + 1]
    c_len, bb, a_rows, d_len = integral_ref.shape

    @pl.when(pl.program_id(0) == 0)
    def _():
        out_ref[...] = jnp.zeros_like(out_ref)

    total = out_ref[...]
    for c in range(c_len):
        taus = [r[c] for r in tau_refs]
        left = taus[0] if count == 1 else jnp.concatenate(taus, axis=0)
        right = integral_ref[c].reshape(bb * a_rows, d_len)
        total += lax.dot_general(left, right, NT, preferred_element_type=jnp.float32)
    out_ref[...] = total


def ladder_terms(taus, integral, c_start):
    c_rows, pairs, d_len = taus[0].shape
    _, bb, a_rows, _ = integral.shape
    c_len = largest_part(c_rows, 4)
    first = c_start // c_len
    count = len(taus)
    return pl.pallas_call(
        functools.partial(ladder_kernel, count),
        grid=(c_rows // c_len,),
        in_specs=[pl.BlockSpec((c_len, pairs, d_len), lambda i: (i, 0, 0))] * count
        + [pl.BlockSpec((c_len, bb, a_rows, d_len), lambda i: (first + i, 0, 0, 0))],
        out_specs=pl.BlockSpec((count * pairs, bb * a_rows), lambda i: (0, 0)),
        out_shape=jax.ShapeDtypeStruct((count * pairs, bb * a_rows), jnp.float32),
        compiler_params=pltpu.CompilerParams(vmem_limit_bytes=32 * 2**20),
        cost_estimate=pl.CostEstimate(
            flops=2 * count * pairs * bb * a_rows * c_rows * d_len,
            bytes_accessed=2 * c_rows * d_len * (count * pairs + bb * a_rows),
            transcendentals=0,
        ),
    )(*taus, integral)


def body(parts, factors, amplitudes):
    a_rows, c_rows, aux_len = factors.shape
    pairs = amplitudes.shape[0]
    n = lax.axis_size("out")
    vir = lax.axis_size("vir")
    z = lax.axis_index("out")

    batch_rows = factors[:BB]
    shared = batch_rows
    for k in range(1, n):
        here = lax.ppermute(batch_rows, "out", [(0, k)])
        shared = jnp.where(z == k, here, shared)
    batch = lax.all_gather(shared, "vir", axis=1, tiled=True)

    piece = c_rows // parts
    own = [
        amplitudes[:, k * piece : (k + 1) * piece].transpose(1, 0, 2) for k in range(parts)
    ]
    ups, downs = [own], [own]
    for s in range(n - 1):
        rise = [(k, k + 1) for k in range(s, n - 1)]
        fall = [(k + 1, k) for k in range(n - 1 - s)]
        ups.append([lax.ppermute(t, "out", rise) for t in ups[-1]])
        downs.append([lax.ppermute(t, "out", fall) for t in downs[-1]])

    integral = integrals(factors, batch)

    def summed(groups):
        return functools.reduce(
            jnp.add, [ladder_terms(list(g), integral, k * piece) for k, g in enumerate(groups)]
        )

    middle = summed([(t,) for t in own])
    both = [summed(zip(ups[s], downs[s])) for s in range(1, n)]
    stacked = jnp.concatenate(
        [t[:pairs] for t in reversed(both)] + [middle] + [t[pairs:] for t in both]
    )
    terms = lax.dynamic_slice_in_dim(stacked, (n - 1 - z) * pairs, n * pairs, axis=0)
    pieces = terms.reshape(vir, n * pairs // vir, BB * a_rows)
    swapped = lax.all_to_all(pieces, "vir", split_axis=0, concat_axis=0)
    out = jnp.sum(swapped, axis=0)
    return out.reshape(-1, BB, a_rows).transpose(1, 0, 2)


def solution(mesh):
    def run(factors, amplitudes):
        c_rows = factors.shape[1] // mesh.shape["vir"]
        parts = 4 if c_rows % 4 == 0 else 1
        placed = (P("out", "vir", None), P("out", "vir", None))
        return jax.shard_map(
            functools.partial(body, parts),
            mesh=mesh,
            in_specs=placed,
            out_specs=P(None, "vir", "out"),
            check_vma=False,
        )(factors, amplitudes)

    return run
```

time: 327 us -> 284 us (0.87)
  waiting for transfers between devices: 217 us -> 71.7 us
  Pallas kernels: 0 us -> 99.6 us
  starting transfers between devices: 0.12 us -> 69.1 us
  matrix products: 63.5 us -> 0 us
  local copies, waits for them, and re-layouts: 28 us -> 16.3 us
  blocking collectives: 0 us -> 9.06 us
    all_gather x2 -> x1, waiting for transfers between devices: 126 us -> 0.01 us  [body(): batch = lax.all_gather(shared, 'vir', axis=1, tiled=True)]
    pallas_call x0 -> x17, Pallas kernels: none -> 99.6 us  [the longest x1 59 us: integrals(): pl.pallas_call(integral_kernel, grid=(a_rows // a_len,), in_specs=[pl.Blo...]
    ppermute x0 -> x27, waiting for transfers between devices: none -> 71.7 us  [the longest x12 43.3 us: body(): ups.append([lax.ppermute(t, 'out', rise) for t in ups[-1]])]
    ppermute x0 -> x27, starting transfers between devices: none -> 69.1 us  [the longest x12 37.9 us: body(): downs.append([lax.ppermute(t, 'out', fall) for t in downs[-1]])]
    dot_general x2 -> x0, matrix products: 63.5 us -> none  [the longest x1 32.4 us: body(): lax.dot_general(local_rows, gathered, (((1,), (2,)), ((), ())), preferred...]
    unnamed x5 -> x1, waiting for transfers between devices: 51.9 us -> 0.02 us
    psum x1 -> x0, waiting for transfers between devices: 39 us -> none  [spread(): return lax.psum(block, axis)]
    convert_element_type x1 -> x0, local copies, waits for them, and re-layouts: 21.3 us -> none  [body(): integral = tiles.astype(jnp.bfloat16).reshape(a_rows, c_rows, BB, piece_len)]
  transfers between devices with their start and end apart: 4 -> 28, of which waited for: 4 -> 11; matrix products, arithmetic and copies ran while one was open for 18% -> 1% of each run, Pallas kernels for 0% -> 27%
where the time goes in v1:
time: 284 us; the launch traced here: 282 us
  Pallas kernels  99.6 us (35%)
  waiting for transfers between devices  71.7 us (25%)
  starting transfers between devices  69.1 us (24%)
  local copies, waits for them, and re-layouts  16.3 us (6%)
  between operations  14 us (5%)
  blocking collectives  9.06 us (3%)
    pallas_call x1, Pallas kernels, integrals(): pl.pallas_call(integral_kernel, grid=(a_rows // a_len,), in_specs=[pl.Blo...  59 us
    ppermute x12, waiting for transfers between devices, body(): ups.append([lax.ppermute(t, 'out', rise) for t in ups[-1]])  43.3 us
    pallas_call x16, Pallas kernels, ladder_terms(): pl.pallas_call(functools.partial(ladder_kernel, count), grid=(c_rows // c...  40.5 us
    ppermute x12, starting transfers between devices, body(): downs.append([lax.ppermute(t, 'out', fall) for t in downs[-1]])  37.9 us
    ppermute x12, starting transfers between devices, body(): ups.append([lax.ppermute(t, 'out', rise) for t in ups[-1]])  28.5 us
    ppermute x3, waiting for transfers between devices, body(): here = lax.ppermute(batch_rows, 'out', [(0, k)])  21.5 us
    unnamed x41, local copies, waits for them, and re-layouts  12.9 us
    all_to_all x1, blocking collectives, body(): swapped = lax.all_to_all(pieces, 'vir', split_axis=0, concat_axis=0)  9.06 us
  transfers between devices with their start and end apart: 28, of which 11 were waited for; matrix products, arithmetic and copies ran while one was open for 1% of the time, Pallas kernels for 27%

profile of v1, /device:TPU:16, one launch (start us, length us, event | category | flops | bytes accessed | tf_op | source)
XLA Modules:
  0.0 281.6 jit_solution(1832595363075373071)
XLA Ops:
  6.5 1.0 slice.34
  8.3 1.3 collective-permute-start.7
  10.3 21.5 %collective-permute-done.7 = bf16[2,64,1536]{2,1,0:T(8,128)(2,1)S(1)} collective-permute-done((bf16[2,64,1536]{2,1,0:T(8,128)(2,1)S(1)}, bf16[2,64,1536]{2,1,0:T(8,128)(2,1)S(1)}, u32[]{:S(2)}, u32[]{:S(2)}) %collective-permute-start.7) | collective-permute-done | bytes 393248 | tf_op jit(solution)/shard_map/ppermute | solution.py:108
  31.8 1.8 select_select_fusion
  33.6 1.7 fusion
  35.7 1.9 collective-permute-start
  37.6 9.7 %collective-permute-start.3 = (bf16[16,32,512]{2,1,0:T(8,128)(2,1)S(1)}, bf16[16,32,512]{2,1,0:T(8,128)(2,1)S(1)}, u32[]{:S(2)}, u32[]{:S(2)}) collective-permute-start(bf16[16,32,512]{2,1,0:T(8,128)(2,1)S(1)} %bitcast.15), channel_id=1, source_target_pairs={{1,0},{2,1},{3,2},{5,4},{6,5},{7,6},{9,8},{10,9},{11,10},{13,12},{... | collective-permute-start | bytes 1572872 | tf_op jit(solution)/shard_map/ppermute | solution.py:121
  47.6 4.0 %collective-permute-start.12 = (bf16[16,32,512]{2,1,0:T(8,128)(2,1)S(1)}, bf16[16,32,512]{2,1,0:T(8,128)(2,1)S(1)}, u32[]{:S(2)}, u32[]{:S(2)}) collective-permute-start(bf16[16,32,512]{2,1,0:T(8,128)(2,1)S(1)} %bitcast.17), channel_id=1, source_target_pairs={{1,0},{2,1},{3,2},{5,4},{6,5},{7,6},{9,8},{10,9},{11,10},{13,12},{... | collective-permute-start | bytes 1572872 | tf_op jit(solution)/shard_map/ppermute | solution.py:121
  51.6 1.9 collective-permute-start.9
  53.8 1.9 collective-permute-start.15
  56.0 2.2 collective-permute-done.refs_0_
  58.2 3.9 %collective-permute-start.18 = (bf16[16,32,512]{2,1,0:T(8,128)(2,1)S(1)}, bf16[16,32,512]{2,1,0:T(8,128)(2,1)S(1)}, u32[]{:S(2)}, u32[]{:S(2)}) collective-permute-start(bf16[16,32,512]{2,1,0:T(8,128)(2,1)S(1)} %bitcast.21), channel_id=1, source_target_pairs={{1,0},{2,1},{3,2},{5,4},{6,5},{7,6},{9,8},{10,9},{11,10},{13,12},{... | collective-permute-start | bytes 1572872 | tf_op jit(solution)/shard_map/ppermute | solution.py:121
  62.2 2.0 collective-permute-start.21
  64.1 6.8 %collective-permute-done.12.refs_1_ = bf16[16,32,512]{2,1,0:T(8,128)(2,1)S(1)} collective-permute-done((bf16[16,32,512]{2,1,0:T(8,128)(2,1)S(1)}, bf16[16,32,512]{2,1,0:T(8,128)(2,1)S(1)}, u32[]{:S(2)}, u32[]{:S(2)}) %collective-permute-start.12) | collective-permute-done | bytes 524320 | tf_op jit(solution)/shard_map/ppermute | solution.py:121
  70.9 4.4 %collective-permute-start.24 = (bf16[16,32,512]{2,1,0:T(8,128)(2,1)S(1)}, bf16[16,32,512]{2,1,0:T(8,128)(2,1)}, u32[]{:S(2)}, u32[]{:S(2)}) collective-permute-start(bf16[16,32,512]{2,1,0:T(8,128)(2,1)S(1)} %bitcast.24), channel_id=1, source_target_pairs={{1,0},{2,1},{3,2},{5,4},{6,5},{7,6},{9,8},{10,9},{11,10},{13,12},{... | collective-permute-start | bytes 1572872 | tf_op jit(solution)/shard_map/ppermute | solution.py:121
  75.3 2.2 collective-permute-start.1
  77.6 3.1 %collective-permute-done.15.refs_0_ = bf16[16,32,512]{2,1,0:T(8,128)(2,1)S(1)} collective-permute-done((bf16[16,32,512]{2,1,0:T(8,128)(2,1)S(1)}, bf16[16,32,512]{2,1,0:T(8,128)(2,1)S(1)}, u32[]{:S(2)}, u32[]{:S(2)}) %collective-permute-start.15) | collective-permute-done | bytes 524320 | tf_op jit(solution)/shard_map/ppermute | solution.py:120
  80.7 4.7 %collective-permute-start.4 = (bf16[16,32,512]{2,1,0:T(8,128)(2,1)S(1)}, bf16[16,32,512]{2,1,0:T(8,128)(2,1)}, u32[]{:S(2)}, u32[]{:S(2)}) collective-permute-start(bf16[16,32,512]{2,1,0:T(8,128)(2,1)S(1)} %collective-permute-done.3.refs_1_), channel_id=1, source_target_pairs={{1,0},{2,1},{5,4},{6,5},{9,8},{10,9},{13,12},{14,13},{17,16},{18,1... | collective-permute-start | bytes 1572872 | tf_op jit(solution)/shard_map/ppermute | solution.py:121
  85.4 1.9 collective-permute-start.10
  87.3 0.8 copy-done.3
  88.1 3.9 %collective-permute-done.21.refs_0_ = bf16[16,32,512]{2,1,0:T(8,128)(2,1)} collective-permute-done((bf16[16,32,512]{2,1,0:T(8,128)(2,1)S(1)}, bf16[16,32,512]{2,1,0:T(8,128)(2,1)}, u32[]{:S(2)}, u32[]{:S(2)}) %collective-permute-start.21) | collective-permute-done | bytes 524320 | tf_op jit(solution)/shard_map/ppermute | solution.py:120
  92.0 1.9 collective-permute-start.13
  93.9 0.8 copy-done.1
  94.7 1.9 collective-permute-start.16
  96.7 0.8 copy-done.5
  97.5 5.8 %collective-permute-done.1.refs_0_ = bf16[16,32,512]{2,1,0:T(8,128)(2,1)} collective-permute-done((bf16[16,32,512]{2,1,0:T(8,128)(2,1)S(1)}, bf16[16,32,512]{2,1,0:T(8,128)(2,1)}, u32[]{:S(2)}, u32[]{:S(2)}) %collective-permute-start.1) | collective-permute-done | bytes 524320 | tf_op jit(solution)/shard_map/ppermute | solution.py:120
  103.3 1.4 collective-permute-start.19
  104.7 0.8 copy-done.7
  105.5 1.9 collective-permute-start.22
  107.4 7.1 %collective-permute-done.10.refs_0_ = bf16[16,32,512]{2,1,0:T(8,128)(2,1)} collective-permute-done((bf16[16,32,512]{2,1,0:T(8,128)(2,1)S(1)}, bf16[16,32,512]{2,1,0:T(8,128)(2,1)}, u32[]{:S(2)}, u32[]{:S(2)}) %collective-permute-start.10) | collective-permute-done | bytes 524320 | tf_op jit(solution)/shard_map/ppermute | solution.py:120
  114.5 2.1 collective-permute-start.25
  116.6 2.1 collective-permute-start.2
  118.8 6.9 %collective-permute-done.16.refs_0_ = bf16[16,32,512]{2,1,0:T(8,128)(2,1)S(1)} collective-permute-done((bf16[16,32,512]{2,1,0:T(8,128)(2,1)S(1)}, bf16[16,32,512]{2,1,0:T(8,128)(2,1)S(1)}, u32[]{:S(2)}, u32[]{:S(2)}) %collective-permute-start.16) | collective-permute-done | bytes 524320 | tf_op jit(solution)/shard_map/ppermute | solution.py:120
  125.6 1.5 collective-permute-start.5
  127.1 0.8 copy-done.13
  127.9 2.1 collective-permute-start.11
  130.0 5.2 %collective-permute-done.22.refs_0_ = bf16[16,32,512]{2,1,0:T(8,128)(2,1)} collective-permute-done((bf16[16,32,512]{2,1,0:T(8,128)(2,1)}, bf16[16,32,512]{2,1,0:T(8,128)(2,1)}, u32[]{:S(2)}, u32[]{:S(2)}) %collective-permute-start.22) | collective-permute-done | bytes 524320 | tf_op jit(solution)/shard_map/ppermute | solution.py:120
  135.2 1.5 collective-permute-start.14
  136.7 3.4 %collective-permute-start.17 = (bf16[16,32,512]{2,1,0:T(8,128)(2,1)}, bf16[16,32,512]{2,1,0:T(8,128)(2,1)}, u32[]{:S(2)}, u32[]{:S(2)}) collective-permute-start(bf16[16,32,512]{2,1,0:T(8,128)(2,1)} %copy-done.11), channel_id=1, source_target_pairs={{2,3},{6,7},{10,11},{14,15},{18,19},{22,23},{26,27},{30,31}} | collective-permute-start | bytes 1572872 | tf_op jit(solution)/shard_map/ppermute | solution.py:120
  140.0 4.6 %collective-permute-done.2.refs_0_ = bf16[16,32,512]{2,1,0:T(8,128)(2,1)} collective-permute-done((bf16[16,32,512]{2,1,0:T(8,128)(2,1)}, bf16[16,32,512]{2,1,0:T(8,128)(2,1)}, u32[]{:S(2)}, u32[]{:S(2)}) %collective-permute-start.2) | collective-permute-done | bytes 524320 | tf_op jit(solution)/shard_map/ppermute | solution.py:120
  144.6 1.5 collective-permute-start.20
  146.1 5.2 %collective-permute-start.23 = (bf16[16,32,512]{2,1,0:T(8,128)(2,1)}, bf16[16,32,512]{2,1,0:T(8,128)(2,1)}, u32[]{:S(2)}, u32[]{:S(2)}) collective-permute-start(bf16[16,32,512]{2,1,0:T(8,128)(2,1)} %collective-permute-done.22.refs_0_), channel_id=1, source_target_pairs={{2,3},{6,7},{10,11},{14,15},{18,19},{22,23},{26,27},{30,31}} | collective-permute-start | bytes 1572872 | tf_op jit(solution)/shard_map/ppermute | solution.py:120
  151.3 4.5 %collective-permute-done.11.refs_0_ = bf16[16,32,512]{2,1,0:T(8,128)(2,1)} collective-permute-done((bf16[16,32,512]{2,1,0:T(8,128)(2,1)}, bf16[16,32,512]{2,1,0:T(8,128)(2,1)}, u32[]{:S(2)}, u32[]{:S(2)}) %collective-permute-start.11) | collective-permute-done | bytes 524320 | tf_op jit(solution)/shard_map/ppermute | solution.py:120
  155.9 1.5 collective-permute-start.26
  157.3 1.9 copy-done.15
  159.2 59.0 %shard_map.28.refs_2_.refs_1_ = bf16[64,2,128,512]{3,2,1,0:T(8,128)(2,1)} custom-call(bf16[128,64,1536]{2,1,0:T(8,128)(2,1)} %factor_ref.1, bf16[2,512,1536]{2,1,0:T(8,128)(2,1)S(1)} %copy-done.15), custom_call_target="tpu_custom_call" | custom-call | flops 25769803776 | bytes 45088768 | tf_op jit(solution)/shard_map/pallas_call | solution.py:40
  218.3 5.8 %copy-done = bf16[64,2,128,512]{3,2,1,0:T(8,128)(2,1)S(1)} copy-done((bf16[64,2,128,512]{3,2,1,0:T(8,128)(2,1)S(1)}, bf16[64,2,128,512]{3,2,1,0:T(8,128)(2,1)}, u32[]{:S(2)}) %copy-start) | copy-done | bytes 16777240
  224.0 1.6 shard_map.41
  225.7 1.7 shard_map.42
  227.4 1.7 shard_map.43
  229.0 1.7 shard_map.44
  230.7 3.3 %shard_map.29 = f32[64,256]{1,0:T(8,128)S(1)} custom-call(bf16[16,32,512]{2,1,0:T(8,128)(2,1)} %collective-permute-done.2.refs_0_, bf16[16,32,512]{2,1,0:T(8,128)(2,1)} %collective-permute-done.5.refs_1_, bf16[64,2,128,512]{3,2,1,0:T(8,128)(2,1)S(1)} %copy-done), custom_call_target="tpu_custom_call" | custom-call | flops 268435456 | bytes 5242880 | tf_op jit(solution)/shard_map/pallas_call | solution.py:82
  234.1 3.3 %shard_map.30 = f32[64,256]{1,0:T(8,128)S(1)} custom-call(bf16[16,32,512]{2,1,0:T(8,128)(2,1)} %collective-permute-done.11.refs_0_, bf16[16,32,512]{2,1,0:T(8,128)(2,1)} %collective-permute-done.14.refs_1_, bf16[64,2,128,512]{3,2,1,0:T(8,128)(2,1)S(1)} %copy-done), custom_call_target="tpu_custom_call" | custom-call | flops 268435456 | bytes 5242880 | tf_op jit(solution)/shard_map/pallas_call | solution.py:82
  237.4 3.3 %shard_map.31 = f32[64,256]{1,0:T(8,128)S(1)} custom-call(bf16[16,32,512]{2,1,0:T(8,128)(2,1)} %collective-permute-done.17.refs_0_, bf16[16,32,512]{2,1,0:T(8,128)(2,1)} %collective-permute-done.20.refs_1_, bf16[64,2,128,512]{3,2,1,0:T(8,128)(2,1)S(1)} %copy-done), custom_call_target="tpu_custom_call" | custom-call | flops 268435456 | bytes 5242880 | tf_op jit(solution)/shard_map/pallas_call | solution.py:82
  240.8 3.4 %shard_map.32 = f32[64,256]{1,0:T(8,128)S(1)} custom-call(bf16[16,32,512]{2,1,0:T(8,128)(2,1)} %collective-permute-done.23.refs_0_, bf16[16,32,512]{2,1,0:T(8,128)(2,1)} %collective-permute-done.26.refs_1_, bf16[64,2,128,512]{3,2,1,0:T(8,128)(2,1)S(1)} %copy-done), custom_call_target="tpu_custom_call" | custom-call | flops 268435456 | bytes 5242880 | tf_op jit(solution)/shard_map/pallas_call | solution.py:82
  244.2 3.4 %shard_map.33 = f32[64,256]{1,0:T(8,128)S(1)} custom-call(bf16[16,32,512]{2,1,0:T(8,128)(2,1)} %collective-permute-done.1.refs_0_, bf16[16,32,512]{2,1,0:T(8,128)(2,1)} %collective-permute-done.4.refs_1_, bf16[64,2,128,512]{3,2,1,0:T(8,128)(2,1)S(1)} %copy-done), custom_call_target="tpu_custom_call" | custom-call | flops 268435456 | bytes 5242880 | tf_op jit(solution)/shard_map/pallas_call | solution.py:82
  247.6 3.2 %shard_map.34 = f32[64,256]{1,0:T(8,128)S(1)} custom-call(bf16[16,32,512]{2,1,0:T(8,128)(2,1)} %collective-permute-done.10.refs_0_, bf16[16,32,512]{2,1,0:T(8,128)(2,1)S(1)} %copy-done.10, bf16[64,2,128,512]{3,2,1,0:T(8,128)(2,1)S(1)} %copy-done), custom_call_target="tpu_custom_call" | custom-call | flops 268435456 | bytes 5242880 | tf_op jit(solution)/shard_map/pallas_call | solution.py:82
  250.8 1.8 shard_map.35
  252.7 3.4 %shard_map.36 = f32[64,256]{1,0:T(8,128)S(1)} custom-call(bf16[16,32,512]{2,1,0:T(8,128)(2,1)} %collective-permute-done.22.refs_0_, bf16[16,32,512]{2,1,0:T(8,128)(2,1)} %collective-permute-done.25.refs_1_, bf16[64,2,128,512]{3,2,1,0:T(8,128)(2,1)S(1)} %copy-done), custom_call_target="tpu_custom_call" | custom-call | flops 268435456 | bytes 5242880 | tf_op jit(solution)/shard_map/pallas_call | solution.py:82
  256.1 1.8 shard_map.37
  258.0 1.8 shard_map.38
  259.8 1.8 shard_map.39
  261.6 3.3 %shard_map.40 = f32[64,256]{1,0:T(8,128)S(1)} custom-call(bf16[16,32,512]{2,1,0:T(8,128)(2,1)} %collective-permute-done.21.refs_0_, bf16[16,32,512]{2,1,0:T(8,128)(2,1)} %collective-permute-done.24.refs_1_, bf16[64,2,128,512]{3,2,1,0:T(8,128)(2,1)S(1)} %copy-done), custom_call_target="tpu_custom_call" | custom-call | flops 268435456 | bytes 5242880 | tf_op jit(solution)/shard_map/pallas_call | solution.py:82
  265.1 9.1 %all_to_all.5 = f32[8,16,256]{2,1,0:T(8,128)S(1)} all-to-all(f32[8,16,256]{2,1,0:T(8,128)S(1)} %bitcast.26), channel_id=1, replica_groups=mesh['vir'=8,'out'=4] {'vir'}, dimensions={0} | all-to-all | bytes 262144 | tf_op jit(solution)/shard_map/all_to_all | solution.py:137
  (64 shorter events, 3.4 us)
Async XLA Ops:
  6.5 150.8 %all-gather.2.cloned.1.call-start = ((), (), s32[]{:S(2)}) async-start(), calls=%async_computation.1 | async-start | bytes 3538944 | tf_op jit(solution)/shard_map/all_gather | solution.py:110
  7.6 2.7 collective-permute-start.6
  8.3 23.5 %collective-permute-start.7 = (bf16[2,64,1536]{2,1,0:T(8,128)(2,1)S(1)}, bf16[2,64,1536]{2,1,0:T(8,128)(2,1)S(1)}, u32[]{:S(2)}, u32[]{:S(2)}) collective-permute-start(bf16[2,64,1536]{2,1,0:T(8,128)(2,1)S(1)} %slice.34), channel_id=1, source_target_pairs={{0,2},{4,6},{8,10},{12,14},{16,18},{20,22},{24,26},{28,30}} | collective-permute-start | bytes 1179656 | tf_op jit(solution)/shard_map/ppermute | solution.py:108
  9.6 22.2 %collective-permute-start.8 = (bf16[2,64,1536]{2,1,0:T(8,128)(2,1)S(1)}, bf16[2,64,1536]{2,1,0:T(8,128)(2,1)S(1)}, u32[]{:S(2)}, u32[]{:S(2)}) collective-permute-start(bf16[2,64,1536]{2,1,0:T(8,128)(2,1)S(1)} %slice.34), channel_id=1, source_target_pairs={{0,1},{4,5},{8,9},{12,13},{16,17},{20,21},{24,25},{28,29}} | collective-permute-start | bytes 1179656 | tf_op jit(solution)/shard_map/ppermute | solution.py:108
  35.7 22.6 %collective-permute-start = (bf16[16,32,512]{2,1,0:T(8,128)(2,1)S(1)}, bf16[16,32,512]{2,1,0:T(8,128)(2,1)S(1)}, u32[]{:S(2)}, u32[]{:S(2)}) collective-permute-start(bf16[16,32,512]{2,1,0:T(8,128)(2,1)S(1)} %bitcast.14), channel_id=1, source_target_pairs={{0,1},{1,2},{2,3},{4,5},{5,6},{6,7},{8,9},{9,10},{10,11},{12,13},{... | collective-permute-start | bytes 1572872 | tf_op jit(solution)/shard_map/ppermute | solution.py:120
  37.6 24.6 %collective-permute-start.3 = (bf16[16,32,512]{2,1,0:T(8,128)(2,1)S(1)}, bf16[16,32,512]{2,1,0:T(8,128)(2,1)S(1)}, u32[]{:S(2)}, u32[]{:S(2)}) collective-permute-start(bf16[16,32,512]{2,1,0:T(8,128)(2,1)S(1)} %bitcast.15), channel_id=1, source_target_pairs={{1,0},{2,1},{3,2},{5,4},{6,5},{7,6},{9,8},{10,9},{11,10},{13,12},{... | collective-permute-start | bytes 1572872 | tf_op jit(solution)/shard_map/ppermute | solution.py:121
  47.6 23.3 %collective-permute-start.12 = (bf16[16,32,512]{2,1,0:T(8,128)(2,1)S(1)}, bf16[16,32,512]{2,1,0:T(8,128)(2,1)S(1)}, u32[]{:S(2)}, u32[]{:S(2)}) collective-permute-start(bf16[16,32,512]{2,1,0:T(8,128)(2,1)S(1)} %bitcast.17), channel_id=1, source_target_pairs={{1,0},{2,1},{3,2},{5,4},{6,5},{7,6},{9,8},{10,9},{11,10},{13,12},{... | collective-permute-start | bytes 1572872 | tf_op jit(solution)/shard_map/ppermute | solution.py:121
  51.6 23.7 %collective-permute-start.9 = (bf16[16,32,512]{2,1,0:T(8,128)(2,1)S(1)}, bf16[16,32,512]{2,1,0:T(8,128)(2,1)S(1)}, u32[]{:S(2)}, u32[]{:S(2)}) collective-permute-start(bf16[16,32,512]{2,1,0:T(8,128)(2,1)S(1)} %bitcast.18), channel_id=1, source_target_pairs={{0,1},{1,2},{2,3},{4,5},{5,6},{6,7},{8,9},{9,10},{10,11},{12,13},{... | collective-permute-start | bytes 1572872 | tf_op jit(solution)/shard_map/ppermute | solution.py:120
  53.8 26.9 %collective-permute-start.15 = (bf16[16,32,512]{2,1,0:T(8,128)(2,1)S(1)}, bf16[16,32,512]{2,1,0:T(8,128)(2,1)S(1)}, u32[]{:S(2)}, u32[]{:S(2)}) collective-permute-start(bf16[16,32,512]{2,1,0:T(8,128)(2,1)S(1)} %bitcast.20), channel_id=1, source_target_pairs={{0,1},{1,2},{2,3},{4,5},{5,6},{6,7},{8,9},{9,10},{10,11},{12,13},{... | collective-permute-start | bytes 1572872 | tf_op jit(solution)/shard_map/ppermute | solution.py:120
  58.2 27.2 %collective-permute-start.18 = (bf16[16,32,512]{2,1,0:T(8,128)(2,1)S(1)}, bf16[16,32,512]{2,1,0:T(8,128)(2,1)S(1)}, u32[]{:S(2)}, u32[]{:S(2)}) collective-permute-start(bf16[16,32,512]{2,1,0:T(8,128)(2,1)S(1)} %bitcast.21), channel_id=1, source_target_pairs={{1,0},{2,1},{3,2},{5,4},{6,5},{7,6},{9,8},{10,9},{11,10},{13,12},{... | collective-permute-start | bytes 1572872 | tf_op jit(solution)/shard_map/ppermute | solution.py:121
  62.2 29.9 %collective-permute-start.21 = (bf16[16,32,512]{2,1,0:T(8,128)(2,1)S(1)}, bf16[16,32,512]{2,1,0:T(8,128)(2,1)}, u32[]{:S(2)}, u32[]{:S(2)}) collective-permute-start(bf16[16,32,512]{2,1,0:T(8,128)(2,1)S(1)} %bitcast.23), channel_id=1, source_target_pairs={{0,1},{1,2},{2,3},{4,5},{5,6},{6,7},{8,9},{9,10},{10,11},{12,13},{... | collective-permute-start | bytes 1572872 | tf_op jit(solution)/shard_map/ppermute | solution.py:120
  70.9 23.8 %collective-permute-start.24 = (bf16[16,32,512]{2,1,0:T(8,128)(2,1)S(1)}, bf16[16,32,512]{2,1,0:T(8,128)(2,1)}, u32[]{:S(2)}, u32[]{:S(2)}) collective-permute-start(bf16[16,32,512]{2,1,0:T(8,128)(2,1)S(1)} %bitcast.24), channel_id=1, source_target_pairs={{1,0},{2,1},{3,2},{5,4},{6,5},{7,6},{9,8},{10,9},{11,10},{13,12},{... | collective-permute-start | bytes 1572872 | tf_op jit(solution)/shard_map/ppermute | solution.py:121
  75.3 28.0 %collective-permute-start.1 = (bf16[16,32,512]{2,1,0:T(8,128)(2,1)S(1)}, bf16[16,32,512]{2,1,0:T(8,128)(2,1)}, u32[]{:S(2)}, u32[]{:S(2)}) collective-permute-start(bf16[16,32,512]{2,1,0:T(8,128)(2,1)S(1)} %collective-permute-done.refs_0_), channel_id=1, source_target_pairs={{1,2},{2,3},{5,6},{6,7},{9,10},{10,11},{13,14},{14,15},{17,18},{18... | collective-permute-start | bytes 1572872 | tf_op jit(solution)/shard_map/ppermute | solution.py:120
  80.7 24.8 %collective-permute-start.4 = (bf16[16,32,512]{2,1,0:T(8,128)(2,1)S(1)}, bf16[16,32,512]{2,1,0:T(8,128)(2,1)}, u32[]{:S(2)}, u32[]{:S(2)}) collective-permute-start(bf16[16,32,512]{2,1,0:T(8,128)(2,1)S(1)} %collective-permute-done.3.refs_1_), channel_id=1, source_target_pairs={{1,0},{2,1},{5,4},{6,5},{9,8},{10,9},{13,12},{14,13},{17,16},{18,1... | collective-permute-start | bytes 1572872 | tf_op jit(solution)/shard_map/ppermute | solution.py:121
  85.4 29.1 %collective-permute-start.10 = (bf16[16,32,512]{2,1,0:T(8,128)(2,1)S(1)}, bf16[16,32,512]{2,1,0:T(8,128)(2,1)}, u32[]{:S(2)}, u32[]{:S(2)}) collective-permute-start(bf16[16,32,512]{2,1,0:T(8,128)(2,1)S(1)} %collective-permute-done.9.refs_0_), channel_id=1, source_target_pairs={{1,2},{2,3},{5,6},{6,7},{9,10},{10,11},{13,14},{14,15},{17,18},{18... | collective-permute-start | bytes 1572872 | tf_op jit(solution)/shard_map/ppermute | solution.py:120
  87.3 0.8 copy-start.3
  92.0 24.6 %collective-permute-start.13 = (bf16[16,32,512]{2,1,0:T(8,128)(2,1)S(1)}, bf16[16,32,512]{2,1,0:T(8,128)(2,1)S(1)}, u32[]{:S(2)}, u32[]{:S(2)}) collective-permute-start(bf16[16,32,512]{2,1,0:T(8,128)(2,1)S(1)} %collective-permute-done.12.refs_1_), channel_id=1, source_target_pairs={{1,0},{2,1},{5,4},{6,5},{9,8},{10,9},{13,12},{14,13},{17,16},{18,1... | collective-permute-start | bytes 1572872 | tf_op jit(solution)/shard_map/ppermute | solution.py:121
  93.9 0.8 copy-start.1
  94.7 30.9 %collective-permute-start.16 = (bf16[16,32,512]{2,1,0:T(8,128)(2,1)S(1)}, bf16[16,32,512]{2,1,0:T(8,128)(2,1)S(1)}, u32[]{:S(2)}, u32[]{:S(2)}) collective-permute-start(bf16[16,32,512]{2,1,0:T(8,128)(2,1)S(1)} %collective-permute-done.15.refs_0_), channel_id=1, source_target_pairs={{1,2},{2,3},{5,6},{6,7},{9,10},{10,11},{13,14},{14,15},{17,18},{18... | collective-permute-start | bytes 1572872 | tf_op jit(solution)/shard_map/ppermute | solution.py:120
  96.7 0.8 copy-start.5
  103.3 23.9 %collective-permute-start.19 = (bf16[16,32,512]{2,1,0:T(8,128)(2,1)S(1)}, bf16[16,32,512]{2,1,0:T(8,128)(2,1)S(1)}, u32[]{:S(2)}, u32[]{:S(2)}) collective-permute-start(bf16[16,32,512]{2,1,0:T(8,128)(2,1)S(1)} %collective-permute-done.18.refs_1_), channel_id=1, source_target_pairs={{1,0},{2,1},{5,4},{6,5},{9,8},{10,9},{13,12},{14,13},{17,16},{18,1... | collective-permute-start | bytes 1572872 | tf_op jit(solution)/shard_map/ppermute | solution.py:121
  104.7 0.8 copy-start.7
  105.5 29.7 %collective-permute-start.22 = (bf16[16,32,512]{2,1,0:T(8,128)(2,1)}, bf16[16,32,512]{2,1,0:T(8,128)(2,1)}, u32[]{:S(2)}, u32[]{:S(2)}) collective-permute-start(bf16[16,32,512]{2,1,0:T(8,128)(2,1)} %collective-permute-done.21.refs_0_), channel_id=1, source_target_pairs={{1,2},{2,3},{5,6},{6,7},{9,10},{10,11},{13,14},{14,15},{17,18},{18... | collective-permute-start | bytes 1572872 | tf_op jit(solution)/shard_map/ppermute | solution.py:120
  114.5 22.1 %collective-permute-start.25 = (bf16[16,32,512]{2,1,0:T(8,128)(2,1)}, bf16[16,32,512]{2,1,0:T(8,128)(2,1)}, u32[]{:S(2)}, u32[]{:S(2)}) collective-permute-start(bf16[16,32,512]{2,1,0:T(8,128)(2,1)} %collective-permute-done.24.refs_1_), channel_id=1, source_target_pairs={{1,0},{2,1},{5,4},{6,5},{9,8},{10,9},{13,12},{14,13},{17,16},{18,1... | collective-permute-start | bytes 1572872 | tf_op jit(solution)/shard_map/ppermute | solution.py:121
  116.6 10.5 %copy-start.9 = (bf16[16,32,512]{2,1,0:T(8,128)(2,1)}, bf16[16,32,512]{2,1,0:T(8,128)(2,1)S(1)}, u32[]{:S(2)}) copy-start(bf16[16,32,512]{2,1,0:T(8,128)(2,1)S(1)} %collective-permute-done.13.refs_1_) | copy-start | bytes 1572868
  116.6 28.0 %collective-permute-start.2 = (bf16[16,32,512]{2,1,0:T(8,128)(2,1)}, bf16[16,32,512]{2,1,0:T(8,128)(2,1)}, u32[]{:S(2)}, u32[]{:S(2)}) collective-permute-start(bf16[16,32,512]{2,1,0:T(8,128)(2,1)} %collective-permute-done.1.refs_0_), channel_id=1, source_target_pairs={{2,3},{6,7},{10,11},{14,15},{18,19},{22,23},{26,27},{30,31}} | collective-permute-start | bytes 1572872 | tf_op jit(solution)/shard_map/ppermute | solution.py:120
  125.6 1.5 copy-start.11
  125.6 20.5 %collective-permute-start.5 = (bf16[16,32,512]{2,1,0:T(8,128)(2,1)}, bf16[16,32,512]{2,1,0:T(8,128)(2,1)}, u32[]{:S(2)}, u32[]{:S(2)}) collective-permute-start(bf16[16,32,512]{2,1,0:T(8,128)(2,1)} %collective-permute-done.4.refs_1_), channel_id=1, source_target_pairs={{1,0},{5,4},{9,8},{13,12},{17,16},{21,20},{25,24},{29,28}} | collective-permute-start | bytes 1572872 | tf_op jit(solution)/shard_map/ppermute | solution.py:121
  127.1 0.8 copy-start.13
  127.9 27.9 %collective-permute-start.11 = (bf16[16,32,512]{2,1,0:T(8,128)(2,1)}, bf16[16,32,512]{2,1,0:T(8,128)(2,1)}, u32[]{:S(2)}, u32[]{:S(2)}) collective-permute-start(bf16[16,32,512]{2,1,0:T(8,128)(2,1)} %collective-permute-done.10.refs_0_), channel_id=1, source_target_pairs={{2,3},{6,7},{10,11},{14,15},{18,19},{22,23},{26,27},{30,31}} | collective-permute-start | bytes 1572872 | tf_op jit(solution)/shard_map/ppermute | solution.py:120
  135.2 98.9 %collective-permute-start.14 = (bf16[16,32,512]{2,1,0:T(8,128)(2,1)}, bf16[16,32,512]{2,1,0:T(8,128)(2,1)}, u32[]{:S(2)}, u32[]{:S(2)}) collective-permute-start(bf16[16,32,512]{2,1,0:T(8,128)(2,1)} %copy-done.9), channel_id=1, source_target_pairs={{1,0},{5,4},{9,8},{13,12},{17,16},{21,20},{25,24},{29,28}} | collective-permute-start | bytes 1572872 | tf_op jit(solution)/shard_map/ppermute | solution.py:121
  136.7 100.7 %collective-permute-start.17 = (bf16[16,32,512]{2,1,0:T(8,128)(2,1)}, bf16[16,32,512]{2,1,0:T(8,128)(2,1)}, u32[]{:S(2)}, u32[]{:S(2)}) collective-permute-start(bf16[16,32,512]{2,1,0:T(8,128)(2,1)} %copy-done.11), channel_id=1, source_target_pairs={{2,3},{6,7},{10,11},{14,15},{18,19},{22,23},{26,27},{30,31}} | collective-permute-start | bytes 1572872 | tf_op jit(solution)/shard_map/ppermute | solution.py:120
  144.6 92.8 %collective-permute-start.20 = (bf16[16,32,512]{2,1,0:T(8,128)(2,1)}, bf16[16,32,512]{2,1,0:T(8,128)(2,1)}, u32[]{:S(2)}, u32[]{:S(2)}) collective-permute-start(bf16[16,32,512]{2,1,0:T(8,128)(2,1)} %copy-done.13), channel_id=1, source_target_pairs={{1,0},{5,4},{9,8},{13,12},{17,16},{21,20},{25,24},{29,28}} | collective-permute-start | bytes 1572872 | tf_op jit(solution)/shard_map/ppermute | solution.py:121
  146.1 94.7 %collective-permute-start.23 = (bf16[16,32,512]{2,1,0:T(8,128)(2,1)}, bf16[16,32,512]{2,1,0:T(8,128)(2,1)}, u32[]{:S(2)}, u32[]{:S(2)}) collective-permute-start(bf16[16,32,512]{2,1,0:T(8,128)(2,1)} %collective-permute-done.22.refs_0_), channel_id=1, source_target_pairs={{2,3},{6,7},{10,11},{14,15},{18,19},{22,23},{26,27},{30,31}} | collective-permute-start | bytes 1572872 | tf_op jit(solution)/shard_map/ppermute | solution.py:120
  155.9 84.9 %collective-permute-start.26 = (bf16[16,32,512]{2,1,0:T(8,128)(2,1)}, bf16[16,32,512]{2,1,0:T(8,128)(2,1)}, u32[]{:S(2)}, u32[]{:S(2)}) collective-permute-start(bf16[16,32,512]{2,1,0:T(8,128)(2,1)} %collective-permute-done.25.refs_1_), channel_id=1, source_target_pairs={{1,0},{5,4},{9,8},{13,12},{17,16},{21,20},{25,24},{29,28}} | collective-permute-start | bytes 1572872 | tf_op jit(solution)/shard_map/ppermute | solution.py:121
  157.3 1.9 copy-start.15
  218.3 5.8 %copy-start = (bf16[64,2,128,512]{3,2,1,0:T(8,128)(2,1)S(1)}, bf16[64,2,128,512]{3,2,1,0:T(8,128)(2,1)}, u32[]{:S(2)}) copy-start(bf16[64,2,128,512]{3,2,1,0:T(8,128)(2,1)} %shard_map.28.refs_2_.refs_1_) | copy-start | bytes 50331652
  240.8 6.9 %copy-start.10 = (bf16[16,32,512]{2,1,0:T(8,128)(2,1)S(1)}, bf16[16,32,512]{2,1,0:T(8,128)(2,1)}, u32[]{:S(2)}) copy-start(bf16[16,32,512]{2,1,0:T(8,128)(2,1)} %copy-done.9) | copy-start | bytes 1572868
  244.2 6.6 %copy-start.12 = (bf16[16,32,512]{2,1,0:T(8,128)(2,1)S(1)}, bf16[16,32,512]{2,1,0:T(8,128)(2,1)}, u32[]{:S(2)}) copy-start(bf16[16,32,512]{2,1,0:T(8,128)(2,1)} %copy-done.11) | copy-start | bytes 1572868
  244.2 6.6 %copy-start.14 = (bf16[16,32,512]{2,1,0:T(8,128)(2,1)S(1)}, bf16[16,32,512]{2,1,0:T(8,128)(2,1)}, u32[]{:S(2)}) copy-start(bf16[16,32,512]{2,1,0:T(8,128)(2,1)} %copy-done.13) | copy-start | bytes 1572868
  252.7 5.3 %copy-start.2 = (bf16[16,32,512]{2,1,0:T(8,128)(2,1)S(1)}, bf16[16,32,512]{2,1,0:T(8,128)(2,1)}, u32[]{:S(2)}) copy-start(bf16[16,32,512]{2,1,0:T(8,128)(2,1)} %copy-done.1) | copy-start | bytes 1572868
  252.7 5.3 %copy-start.4 = (bf16[16,32,512]{2,1,0:T(8,128)(2,1)S(1)}, bf16[16,32,512]{2,1,0:T(8,128)(2,1)}, u32[]{:S(2)}) copy-start(bf16[16,32,512]{2,1,0:T(8,128)(2,1)} %copy-done.3) | copy-start | bytes 1572868
  256.1 3.7 %copy-start.6 = (bf16[16,32,512]{2,1,0:T(8,128)(2,1)S(1)}, bf16[16,32,512]{2,1,0:T(8,128)(2,1)}, u32[]{:S(2)}) copy-start(bf16[16,32,512]{2,1,0:T(8,128)(2,1)} %copy-done.5) | copy-start | bytes 1572868
  256.1 3.7 %copy-start.8 = (bf16[16,32,512]{2,1,0:T(8,128)(2,1)S(1)}, bf16[16,32,512]{2,1,0:T(8,128)(2,1)}, u32[]{:S(2)}) copy-start(bf16[16,32,512]{2,1,0:T(8,128)(2,1)} %copy-done.7) | copy-start | bytes 1572868
Sparse Core Ops, SparseCore 0:
  33.8 38.7 all-gather.1

commit v2 on v1

v2 whole, which is shorter than its diff:
```python
import functools

import jax
import jax.numpy as jnp
from jax import lax
from jax.experimental import pallas as pl
from jax.experimental.pallas import tpu as pltpu
from jax.sharding import PartitionSpec as P

BB = 2
LANES = 128
NT = (((1,), (1,)), ((), ()))
NN = (((1,), (0,)), ((), ()))
LITTLE = pl.CostEstimate(flops=1024, bytes_accessed=1024, transcendentals=0)


def largest_part(extent, limit):
    part = min(extent, limit)
    while extent % part:
        part -= 1
    return part


def call(kernel, inputs, in_specs, out_shape, out_spec, through, grid=(1,), scratch=(), into=None):
    n_in, n_thru = len(inputs), len(through)
    kept = [] if into is None else [into]

    def run(*refs):
        outs = refs[n_in + len(kept) + n_thru :]
        kernel(*refs[:n_in], outs[0], *outs[1 + n_thru :])

    anywhere = pl.BlockSpec(memory_space=pl.ANY)
    first = n_in + len(kept)
    aliases = {first + k: 1 + k for k in range(n_thru)}
    if kept:
        aliases[n_in] = 0
    out = pl.pallas_call(
        run,
        grid=grid,
        in_specs=list(in_specs) + [anywhere] * (len(kept) + n_thru),
        out_specs=[out_spec] + [anywhere] * n_thru,
        out_shape=[out_shape] + [jax.ShapeDtypeStruct(t.shape, t.dtype) for t in through],
        input_output_aliases=aliases,
        scratch_shapes=list(scratch),
        compiler_params=pltpu.CompilerParams(vmem_limit_bytes=48 * 2**20),
        cost_estimate=LITTLE,
    )(*inputs, *kept, *through)
    return out[0], list(out[1:])


def fence(arrays):
    def nothing(*refs):
        pass

    anywhere = [pl.BlockSpec(memory_space=pl.ANY)] * len(arrays)
    return list(
        pl.pallas_call(
            nothing,
            in_specs=anywhere,
            out_specs=anywhere,
            out_shape=[jax.ShapeDtypeStruct(t.shape, t.dtype) for t in arrays],
            input_output_aliases={k: k for k in range(len(arrays))},
            cost_estimate=LITTLE,
        )(*arrays)
    )


def turn_kernel(batch_ref, out_ref):
    for b in range(out_ref.shape[0]):
        out_ref[b] = batch_ref[b].T


def turn(batch, through):
    bb, d_len, aux_len = batch.shape
    vmem = pl.BlockSpec(memory_space=pltpu.VMEM)
    out_shape = jax.ShapeDtypeStruct((bb, aux_len, d_len), jnp.bfloat16)
    return call(turn_kernel, [batch], [vmem], out_shape, vmem, through)


def integral_kernel(factor_ref, batch_ref, out_ref):
    a_len, c_len, aux_len = factor_ref.shape
    d_len = out_ref.shape[3]
    rows = factor_ref[...].reshape(a_len * c_len, aux_len)
    wide = largest_part(d_len // LANES, 2) * LANES
    for b in range(out_ref.shape[1]):
        for j in range(0, d_len, wide):
            tile = lax.dot_general(
                rows, batch_ref[b, :, j : j + wide], NN, preferred_element_type=jnp.float32
            )
            turned = jnp.swapaxes(tile.reshape(a_len, c_len, wide), 0, 1)
            out_ref[:, b, :, j : j + wide] = turned.astype(jnp.bfloat16)


def integrals(factors, batch, part, parts, through, into):
    a_rows, c_rows, aux_len = factors.shape
    bb, _, d_len = batch.shape
    c_len = c_rows // parts
    a_len = largest_part(a_rows, 16)
    return call(
        integral_kernel,
        [factors, batch],
        [
            pl.BlockSpec((a_len, c_len, aux_len), lambda i: (i, part, 0)),
            pl.BlockSpec((bb, aux_len, d_len), lambda i: (0, 0, 0)),
        ],
        jax.ShapeDtypeStruct((c_rows, bb, a_rows, d_len), jnp.bfloat16),
        pl.BlockSpec((c_len, bb, a_len, d_len), lambda i: (part, 0, i, 0)),
        through,
        grid=(a_rows // a_len,),
        into=into,
    )


def ladder_kernel(count, *refs):
    tau_refs, integral_ref, out_ref = refs[:count], refs[count], refs[count + 1]
    c_len, bb, a_rows, d_len = integral_ref.shape

    @pl.when(pl.program_id(0) == 0)
    def _():
        out_ref[...] = jnp.zeros_like(out_ref)

    total = out_ref[...]
    for c in range(c_len):
        taus = [r[c] for r in tau_refs]
        left = taus[0] if count == 1 else jnp.concatenate(taus, axis=0)
        right = integral_ref[c].reshape(bb * a_rows, d_len)
        total += lax.dot_general(left, right, NT, preferred_element_type=jnp.float32)
    out_ref[...] = total


def ladder_terms(taus, integral, c_start, through):
    c_rows, pairs, d_len = taus[0].shape
    _, bb, a_rows, _ = integral.shape
    c_len = largest_part(c_rows, 4)
    first = c_start // c_len
    count = len(taus)
    return call(
        functools.partial(ladder_kernel, count),
        list(taus) + [integral],
        [pl.BlockSpec((c_len, pairs, d_len), lambda i: (i, 0, 0))] * count
        + [pl.BlockSpec((c_len, bb, a_rows, d_len), lambda i: (first + i, 0, 0, 0))],
        jax.ShapeDtypeStruct((count * pairs, bb * a_rows), jnp.float32),
        pl.BlockSpec((count * pairs, bb * a_rows), lambda i: (0, 0)),
        through,
        grid=(c_rows // c_len,),
    )


def body(pieces, slices, factors, amplitudes):
    a_rows, c_rows, _ = factors.shape
    pairs = amplitudes.shape[0]
    n = lax.axis_size("out")
    vir = lax.axis_size("vir")
    z = lax.axis_index("out")
    piece = c_rows // pieces
    last = (n - 1) * pieces

    token = [jnp.zeros((8, LANES), jnp.float32)]
    batch_rows = factors[:BB]
    heres = [lax.ppermute(batch_rows, "out", [(0, k)]) for k in range(1, n)]

    arrived = []
    for k in range(pieces):
        own = amplitudes[:, k * piece : (k + 1) * piece].transpose(1, 0, 2)
        arrived.append([own, own])

    def send(upto):
        while len(arrived) < min(upto, last) + pieces:
            step = len(arrived) // pieces
            rise = [(k, k + 1) for k in range(step - 1, n - 1)]
            fall = [(k + 1, k) for k in range(n - step)]
            up, down = arrived[-pieces]
            arrived.append([lax.ppermute(up, "out", rise), lax.ppermute(down, "out", fall)])

    def ordered(step, items, others=()):
        items = [i + pieces for i in items if i < last - pieces]
        through = token + [t for i in items for t in arrived[i]]
        made, passed = step(through + list(others))
        token[0] = passed[0]
        for k, i in enumerate(items):
            arrived[i] = passed[1 + 2 * k : 3 + 2 * k]
        return made, passed[1 + 2 * len(items) :]

    downs = [(k + 1, k) for k in range(n - 1)]
    top = lax.ppermute(arrived[0][0], "out", [(n - 2, n - 1)])
    fallen = lax.ppermute(arrived[0][1], "out", downs)
    _, passed = ordered(lambda t: (None, fence(t)), [], heres + [top, fallen])
    heres, (top, fallen) = passed[: n - 1], passed[n - 1 :]
    shared = batch_rows
    for k in range(1, n):
        shared = jnp.where(z == k, heres[k - 1], shared)
    gathered = lax.all_gather(shared, "vir", axis=1, tiled=True)
    risen = lax.ppermute(arrived[0][0], "out", [(k, k + 1) for k in range(n - 2)])
    arrived.append([jnp.where(z == n - 1, top, risen), fallen])
    send(pieces)
    ordered(lambda t: (None, fence(t)), [0])
    send(pieces + 1)
    batch, _ = ordered(lambda t: turn(gathered, t), [1])
    send(pieces + 2)

    integral = None
    for q in range(slices):
        item = [pieces] if q == slices - 2 else []
        integral, _ = ordered(
            lambda t: integrals(factors, batch, q, slices, t, integral), item
        )
        if item:
            send(2 * pieces + 1)
    done = len(arrived) - 2 * pieces
    while done < (n - 3) * pieces + 1:
        ordered(lambda t: (None, fence(t)), [done])
        done += 1
        send(done + pieces)

    def taus(steps, k):
        return [t for s in steps for t in (arrived[s * pieces + k][:1] if s == 0 else arrived[s * pieces + k])]

    before = []
    for k in range(pieces):
        items = [done] if done < (n - 2) * pieces and done % pieces != k else []
        made, _ = ordered(
            lambda t: ladder_terms(taus(range(n - 1), k), integral, k * piece, t), items
        )
        before.append(made)
        done += 1
        send(done + pieces)
    after = [
        ordered(lambda t: ladder_terms(taus([n - 1], k), integral, k * piece, t), [])[0]
        for k in range(pieces)
    ]
    early = functools.reduce(jnp.add, before)
    late = functools.reduce(jnp.add, after)

    blocks = {0: early[:pairs]}
    for s in range(1, n):
        pair = late if s == n - 1 else early[(2 * s - 1) * pairs : (2 * s + 1) * pairs]
        blocks[-s], blocks[s] = pair[:pairs], pair[pairs:]
    stacked = jnp.concatenate([blocks[s] for s in range(1 - n, n)])
    terms = lax.dynamic_slice_in_dim(stacked, (n - 1 - z) * pairs, n * pairs, axis=0)
    parts = terms.reshape(vir, n * pairs // vir, BB * a_rows)
    swapped = lax.all_to_all(parts, "vir", split_axis=0, concat_axis=0)
    out = jnp.sum(swapped, axis=0)
    return out.reshape(-1, BB, a_rows).transpose(1, 0, 2)


def solution(mesh):
    def run(factors, amplitudes):
        c_rows = factors.shape[1] // mesh.shape["vir"]
        pieces = 2 if c_rows % 2 == 0 else 1
        slices = 4 if c_rows % 32 == 0 else 1
        placed = (P("out", "vir", None), P("out", "vir", None))
        return jax.shard_map(
            functools.partial(body, pieces, slices),
            mesh=mesh,
            in_specs=placed,
            out_specs=P(None, "vir", "out"),
            check_vma=False,
        )(factors, amplitudes)

    return run
```

time: 284 us -> 215 us (0.76)
  starting transfers between devices: 69.1 us -> 37.4 us
  Pallas kernels: 99.6 us -> 80.8 us
  waiting for transfers between devices: 71.7 us -> 55.7 us
  local copies, waits for them, and re-layouts: 16.3 us -> 13.2 us
    ppermute x27 -> x16, starting transfers between devices: 69.1 us -> 37.4 us  [the longest x5 15.1 us: send(): lax.ppermute(down, 'out', fall)]
    pallas_call x17 -> x11, Pallas kernels: 99.6 us -> 80.8 us  [the longest x9 80.8 us: call(): pl.pallas_call(run, grid=grid, in_specs=list(in_specs) + [anywhere] * (le...]
    ppermute x27 -> x16, waiting for transfers between devices: 71.7 us -> 55.7 us  [the longest x1 17.4 us: body(): lax.ppermute(arrived[0][0], 'out', [(k, k + 1) for k in range(n - 2)])]
    unnamed x41 -> x34, local copies, waits for them, and re-layouts: 12.9 us -> 7.4 us
  transfers between devices with their start and end apart: 28 -> 17, of which waited for: 11 -> 4; matrix products, arithmetic and copies ran while one was open for 1% -> 2% of each run, Pallas kernels for 27% -> 34%
where the time goes in v2:
time: 215 us; the launch traced here: 213 us
  Pallas kernels  80.8 us (38%)
  waiting for transfers between devices  55.7 us (26%)
  starting transfers between devices  37.4 us (17%)
  between operations  13.7 us (6%)
  local copies, waits for them, and re-layouts  13.2 us (6%)
  blocking collectives  9.06 us (4%)
  other arithmetic  3.09 us (1%)
    pallas_call x9, Pallas kernels, call(): pl.pallas_call(run, grid=grid, in_specs=list(in_specs) + [anywhere] * (le...  80.8 us
    ppermute x1, waiting for transfers between devices, body(): lax.ppermute(arrived[0][0], 'out', [(k, k + 1) for k in range(n - 2)])  17.4 us
    ppermute x3, waiting for transfers between devices, body(): heres = [lax.ppermute(batch_rows, 'out', [(0, k)]) for k in range(1, n)]  16.3 us
    ppermute x5, starting transfers between devices, send(): lax.ppermute(down, 'out', fall)  15.1 us
    ppermute x5, waiting for transfers between devices, send(): lax.ppermute(up, 'out', rise)  14.6 us
    ppermute x5, starting transfers between devices, send(): lax.ppermute(up, 'out', rise)  12.2 us
    all_to_all x1, blocking collectives, body(): swapped = lax.all_to_all(parts, 'vir', split_axis=0, concat_axis=0)  9.06 us
    unnamed x34, local copies, waits for them, and re-layouts  7.4 us
  transfers between devices with their start and end apart: 17, of which 4 were waited for; matrix products, arithmetic and copies ran while one was open for 2% of the time, Pallas kernels for 34%

profile of v2, /device:TPU:16, one launch (start us, length us, event | category | flops | bytes accessed | tf_op | source)
XLA Modules:
  0.0 213.0 jit_solution(5956276164947083081)
XLA Ops:
  6.5 0.0 all-gather.2.cloned.1.call-start
  6.5 2.8 %fusion = (bf16[32,32,512]{2,1,0:T(8,128)(2,1)}, bf16[32,32,512]{2,1,0:T(8,128)(2,1)S(1)}) fusion(bf16[32,64,512]{2,1,0:T(8,128)(2,1)} %param.3), kind=kLoop, calls=%fused_computation.12 | loop fusion | bytes 4194304 | tf_op jit(solution)/shard_map/slice | solution.py:164
  9.3 0.6 copy.40
  9.9 3.5 %collective-permute-start.3 = (bf16[32,32,512]{2,1,0:T(8,128)(2,1)S(1)}, bf16[32,32,512]{2,1,0:T(8,128)(2,1)S(1)}, u32[]{:S(2)}, u32[]{:S(2)}) collective-permute-start(bf16[32,32,512]{2,1,0:T(8,128)(2,1)S(1)} %bitcast.8), channel_id=1, source_target_pairs={{2,3},{6,7},{10,11},{14,15},{18,19},{22,23},{26,27},{30,31}} | collective-permute-start | bytes 3145736 | tf_op jit(solution)/shard_map/ppermute | solution.py:185
  13.5 1.9 collective-permute-start.4
  15.4 1.8 slice.36
  17.2 0.7 collective-permute-start
  17.9 1.3 collective-permute-start.1
  19.2 1.4 collective-permute-start.2
  20.6 0.0 collective-permute-done.refs_1_
  20.6 16.3 %collective-permute-done.1.refs_2_ = bf16[2,64,1536]{2,1,0:T(8,128)(2,1)} collective-permute-done((bf16[2,64,1536]{2,1,0:T(8,128)(2,1)}, bf16[2,64,1536]{2,1,0:T(8,128)(2,1)}, u32[]{:S(2)}, u32[]{:S(2)}) %collective-permute-start.1) | collective-permute-done | bytes 393248 | tf_op jit(solution)/shard_map/ppermute | solution.py:160
  36.9 0.0 collective-permute-done.2.refs_3_
  36.9 7.4 %collective-permute-done.3.refs_4_ = bf16[32,32,512]{2,1,0:T(8,128)(2,1)S(1)} collective-permute-done((bf16[32,32,512]{2,1,0:T(8,128)(2,1)S(1)}, bf16[32,32,512]{2,1,0:T(8,128)(2,1)S(1)}, u32[]{:S(2)}, u32[]{:S(2)}) %collective-permute-start.3) | collective-permute-done | bytes 1048608 | tf_op jit(solution)/shard_map/ppermute | solution.py:185
  44.2 0.0 collective-permute-done.4.refs_5_
  44.2 0.6 broadcast_in_dim.3.refs_0_
  44.9 0.0 copy-done.12
  44.9 0.4 copy-done.11
  45.2 0.5 copy-done
  45.7 1.9 select_select_fusion
  47.6 0.0 all-gather.2.cloned.1.call-update
  47.7 1.3 collective-permute-start.5
  49.0 1.0 copy-done.4
  49.9 1.8 copy.39
  51.7 3.8 %collective-permute-start.6 = (bf16[32,32,512]{2,1,0:T(8,128)(2,1)S(1)}, bf16[32,32,512]{2,1,0:T(8,128)(2,1)}, u32[]{:S(2)}, u32[]{:S(2)}) collective-permute-start(bf16[32,32,512]{2,1,0:T(8,128)(2,1)S(1)} %bitcast.12), channel_id=1, source_target_pairs={{0,1},{1,2},{2,3},{4,5},{5,6},{6,7},{8,9},{9,10},{10,11},{12,13},{... | collective-permute-start | bytes 3145736 | tf_op jit(solution)/shard_map/ppermute | solution.py:173
  55.6 2.6 %collective-permute-start.7 = (bf16[32,32,512]{2,1,0:T(8,128)(2,1)S(1)}, bf16[32,32,512]{2,1,0:T(8,128)(2,1)}, u32[]{:S(2)}, u32[]{:S(2)}) collective-permute-start(bf16[32,32,512]{2,1,0:T(8,128)(2,1)S(1)} %bitcast.13), channel_id=1, source_target_pairs={{1,0},{2,1},{3,2},{5,4},{6,5},{7,6},{9,8},{10,9},{11,10},{13,12},{... | collective-permute-start | bytes 3145736 | tf_op jit(solution)/shard_map/ppermute | solution.py:173
  58.2 17.4 %collective-permute-done.5 = bf16[32,32,512]{2,1,0:T(8,128)(2,1)S(1)} collective-permute-done((bf16[32,32,512]{2,1,0:T(8,128)(2,1)S(1)}, bf16[32,32,512]{2,1,0:T(8,128)(2,1)S(1)}, u32[]{:S(2)}, u32[]{:S(2)}) %collective-permute-start.5) | collective-permute-done | bytes 1048608 | tf_op jit(solution)/shard_map/ppermute | solution.py:193
  75.6 1.1 broadcast_select_fusion.refs_1_
  76.7 1.9 collective-permute-start.8
  78.7 5.0 %collective-permute-start.9 = (bf16[32,32,512]{2,1,0:T(8,128)(2,1)}, bf16[32,32,512]{2,1,0:T(8,128)(2,1)}, u32[]{:S(2)}, u32[]{:S(2)}) collective-permute-start(bf16[32,32,512]{2,1,0:T(8,128)(2,1)} %get-tuple-element.51.refs_2_), channel_id=1, source_target_pairs={{1,0},{2,1},{5,4},{6,5},{9,8},{10,9},{13,12},{14,13},{17,16},{18,1... | collective-permute-start | bytes 3145736 | tf_op jit(solution)/shard_map/ppermute | solution.py:173
  83.6 14.6 %collective-permute-done.6.refs_2_ = bf16[32,32,512]{2,1,0:T(8,128)(2,1)} collective-permute-done((bf16[32,32,512]{2,1,0:T(8,128)(2,1)S(1)}, bf16[32,32,512]{2,1,0:T(8,128)(2,1)}, u32[]{:S(2)}, u32[]{:S(2)}) %collective-permute-start.6) | collective-permute-done | bytes 1048608 | tf_op jit(solution)/shard_map/ppermute | solution.py:173
  98.2 0.0 collective-permute-done.7.refs_3_
  98.2 0.7 copy-done.8
  98.9 2.7 %shard_map.30 = (bf16[2,1536,512]{2,1,0:T(8,128)(2,1)S(1)}, f32[8,128]{1,0:T(8,128)S(1)}, bf16[32,32,512]{2,1,0:T(8,128)(2,1)}, bf16[32,32,512]{2,1,0:T(8,128)(2,1)}) custom-call(bf16[2,512,1536]{2,1,0:T(8,128)(2,1)} %all-gather.2.cloned.1.call-done.refs_0_, f32[8,128]{1,0:T(8,128)S(1)} %copy-done.8, ...), custom_call_target="tpu_custom_call", output_to_operand_aliasing={{1}: (1, {}), {2}: (2, {}), {3}: (3, {})} | custom-call | flops 1024 | bytes 1024 | tf_op jit(solution)/shard_map/pallas_call | solution.py:37
  101.7 0.0 copy-done.6
  101.7 1.9 collective-permute-start.12
  103.6 4.0 %collective-permute-start.13 = (bf16[32,32,512]{2,1,0:T(8,128)(2,1)}, bf16[32,32,512]{2,1,0:T(8,128)(2,1)S(1)}, u32[]{:S(2)}, u32[]{:S(2)}) collective-permute-start(bf16[32,32,512]{2,1,0:T(8,128)(2,1)} %get-tuple-element.58.refs_2_), channel_id=1, source_target_pairs={{1,0},{2,1},{5,4},{6,5},{9,8},{10,9},{13,12},{14,13},{17,16},{18,1... | collective-permute-start | bytes 3145736 | tf_op jit(solution)/shard_map/ppermute | solution.py:173
  107.7 11.5 %shard_map.31 = (bf16[64,2,128,512]{3,2,1,0:T(8,128)(2,1)}, f32[8,128]{1,0:T(8,128)S(1)}) custom-call(bf16[128,64,1536]{2,1,0:T(8,128)(2,1)} %refs_0_.7, bf16[2,1536,512]{2,1,0:T(8,128)(2,1)S(1)} %get-tuple-element.44.refs_1_, f32[8,128]{1,0:T(8,128)S(1)} %get-tuple-element.45.refs_2_), custom_call_target="tpu_custom_call", output_to_operand_aliasing={{1}: (2, {})} | custom-call | flops 1024 | bytes 1024 | tf_op jit(solution)/shard_map/pallas_call | solution.py:37
  119.2 11.5 %shard_map.32 = (bf16[64,2,128,512]{3,2,1,0:T(8,128)(2,1)}, f32[8,128]{1,0:T(8,128)S(1)}) custom-call(bf16[128,64,1536]{2,1,0:T(8,128)(2,1)} %refs_0_.7, bf16[2,1536,512]{2,1,0:T(8,128)(2,1)S(1)} %get-tuple-element.44.refs_1_, bf16[64,2,128,512]{3,2,1,0:T(8,128)(2,1)} %get-tuple-element.46.refs_2_, ...), custom_call_target="tpu_custom_call", output_to_operand_aliasing={{1}: (3, {}), {0}: (2, {})} | custom-call | flops 1024 | bytes 1024 | tf_op jit(solution)/shard_map/pallas_call | solution.py:37
  130.6 0.0 collective-permute-done.8.refs_4_
  130.6 0.0 collective-permute-done.9.refs_5_
  130.6 11.5 %shard_map.33 = (bf16[64,2,128,512]{3,2,1,0:T(8,128)(2,1)}, f32[8,128]{1,0:T(8,128)S(1)}, bf16[32,32,512]{2,1,0:T(8,128)(2,1)S(1)}, bf16[32,32,512]{2,1,0:T(8,128)(2,1)}) custom-call(bf16[128,64,1536]{2,1,0:T(8,128)(2,1)} %refs_0_.7, ...), custom_call_target="tpu_custom_call", output_to_operand_aliasing={{1}: (3, {}), {2}: (4, {}), {3}: (5, {}), {0}: (2, {})} | custom-call | flops 1024 | bytes 1024 | tf_op jit(solution)/shard_map/pallas_call | solution.py:37
  142.1 2.3 %collective-permute-start.10 = (bf16[32,32,512]{2,1,0:T(8,128)(2,1)S(1)}, bf16[32,32,512]{2,1,0:T(8,128)(2,1)}, u32[]{:S(2)}, u32[]{:S(2)}) collective-permute-start(bf16[32,32,512]{2,1,0:T(8,128)(2,1)S(1)} %get-tuple-element.52.refs_3_), channel_id=1, source_target_pairs={{2,3},{6,7},{10,11},{14,15},{18,19},{22,23},{26,27},{30,31}} | collective-permute-start | bytes 3145736 | tf_op jit(solution)/shard_map/ppermute | solution.py:173
  144.4 1.7 collective-permute-start.11
  146.1 11.7 %shard_map.34 = (bf16[64,2,128,512]{3,2,1,0:T(8,128)(2,1)}, f32[8,128]{1,0:T(8,128)S(1)}) custom-call(bf16[128,64,1536]{2,1,0:T(8,128)(2,1)} %refs_0_.7, bf16[2,1536,512]{2,1,0:T(8,128)(2,1)S(1)} %get-tuple-element.44.refs_1_, bf16[64,2,128,512]{3,2,1,0:T(8,128)(2,1)} %get-tuple-element.54.refs_2_, ...), custom_call_target="tpu_custom_call", output_to_operand_aliasing={{1}: (3, {}), {0}: (2, {})} | custom-call | flops 1024 | bytes 1024 | tf_op jit(solution)/shard_map/pallas_call | solution.py:37
  157.7 0.0 collective-permute-done.12.refs_7_
  157.7 0.0 collective-permute-done.13.refs_8_
  157.7 0.0 copy-done.1
  157.7 0.0 copy-done.2
  157.8 8.1 %shard_map.35 = (f32[160,256]{1,0:T(8,128)S(1)}, f32[8,128]{1,0:T(8,128)S(1)}, bf16[32,32,512]{2,1,0:T(8,128)(2,1)S(1)}, bf16[32,32,512]{2,1,0:T(8,128)(2,1)S(1)}) custom-call(bf16[32,32,512]{2,1,0:T(8,128)(2,1)S(1)} %bitcast.11, bf16[32,32,512]{2,1,0:T(8,128)(2,1)S(1)} %copy-done.2, ...), custom_call_target="tpu_custom_call", output_to_operand_aliasing={{1}: (6, {}), {2}: (7, {}), {3}: (8, {})} | custom-call | flops 1024 | bytes 1024 | tf_op jit(solution)/shard_map/pallas_call | solution.py:37
  165.9 0.0 copy-start.9
  165.9 0.6 copy-done.9
  166.5 2.3 %collective-permute-start.14 = (bf16[32,32,512]{2,1,0:T(8,128)(2,1)S(1)}, bf16[32,32,512]{2,1,0:T(8,128)(2,1)}, u32[]{:S(2)}, u32[]{:S(2)}) collective-permute-start(bf16[32,32,512]{2,1,0:T(8,128)(2,1)S(1)} %get-tuple-element.60.refs_3_), channel_id=1, source_target_pairs={{2,3},{6,7},{10,11},{14,15},{18,19},{22,23},{26,27},{30,31}} | collective-permute-start | bytes 3145736 | tf_op jit(solution)/shard_map/ppermute | solution.py:173
  168.8 1.7 collective-permute-start.15
  170.5 1.2 copy-done.7
  171.7 0.7 copy-done.10
  172.4 8.1 %shard_map.36 = (f32[160,256]{1,0:T(8,128)S(1)}, f32[8,128]{1,0:T(8,128)S(1)}) custom-call(bf16[32,32,512]{2,1,0:T(8,128)(2,1)S(1)} %bitcast.14, bf16[32,32,512]{2,1,0:T(8,128)(2,1)} %get-tuple-element.57.refs_1_, bf16[32,32,512]{2,1,0:T(8,128)(2,1)} %get-tuple-element.58.refs_2_, ...), custom_call_target="tpu_custom_call", output_to_operand_aliasing={{1}: (6, {})} | custom-call | flops 1024 | bytes 1024 | tf_op jit(solution)/shard_map/pallas_call | solution.py:37
  180.5 0.0 collective-permute-done.10.refs_0_
  180.5 0.0 collective-permute-done.11.refs_1_
  180.6 7.8 %shard_map.37 = (f32[64,256]{1,0:T(8,128)S(1)}, f32[8,128]{1,0:T(8,128)S(1)}) custom-call(bf16[32,32,512]{2,1,0:T(8,128)(2,1)} %collective-permute-done.10.refs_0_, bf16[32,32,512]{2,1,0:T(8,128)(2,1)} %collective-permute-done.11.refs_1_, bf16[64,2,128,512]{3,2,1,0:T(8,128)(2,1)} %get-tuple-element.56.refs_5_.refs_2_, ...), custom_call_target="tpu_custom_call", output_to_operand_aliasing={{1}: (3, {})} | custom-call | flops 1024 | bytes 1024 | tf_op jit(solution)/shard_map/pallas_call | solution.py:37
  188.4 0.0 collective-permute-done.14.refs_0_
  188.4 0.0 collective-permute-done.15.refs_1_
  188.4 7.8 %shard_map.38 = (f32[64,256]{1,0:T(8,128)S(1)}, f32[8,128]{1,0:T(8,128)S(1)}) custom-call(bf16[32,32,512]{2,1,0:T(8,128)(2,1)} %collective-permute-done.14.refs_0_, bf16[32,32,512]{2,1,0:T(8,128)(2,1)} %collective-permute-done.15.refs_1_, bf16[64,2,128,512]{3,2,1,0:T(8,128)(2,1)} %get-tuple-element.56.refs_5_.refs_2_, ...), custom_call_target="tpu_custom_call", output_to_operand_aliasing={{1}: (3, {})} | custom-call | flops 1024 | bytes 1024 | tf_op jit(solution)/shard_map/pallas_call | solution.py:37
  196.4 9.1 %all_to_all.5 = f32[8,16,256]{2,1,0:T(8,128)S(1)} all-to-all(f32[8,16,256]{2,1,0:T(8,128)S(1)} %bitcast.15), channel_id=1, replica_groups=mesh['vir'=8,'out'=4] {'vir'}, dimensions={0} | all-to-all | bytes 262144 | tf_op jit(solution)/shard_map/all_to_all | solution.py:241
  205.5 0.6 copy.34
  (29 shorter events, 0.1 us)
Async XLA Ops:
  6.5 91.7 %all-gather.2.cloned.1.call-start = ((), (), s32[]{:S(2)}) async-start(), calls=%async_computation.1 | async-start | bytes 3538944 | tf_op jit(solution)/shard_map/all_gather | solution.py:192
  9.9 34.3 %collective-permute-start.3 = (bf16[32,32,512]{2,1,0:T(8,128)(2,1)S(1)}, bf16[32,32,512]{2,1,0:T(8,128)(2,1)S(1)}, u32[]{:S(2)}, u32[]{:S(2)}) collective-permute-start(bf16[32,32,512]{2,1,0:T(8,128)(2,1)S(1)} %bitcast.8), channel_id=1, source_target_pairs={{2,3},{6,7},{10,11},{14,15},{18,19},{22,23},{26,27},{30,31}} | collective-permute-start | bytes 3145736 | tf_op jit(solution)/shard_map/ppermute | solution.py:185
  13.5 30.8 %collective-permute-start.4 = (bf16[32,32,512]{2,1,0:T(8,128)(2,1)S(1)}, bf16[32,32,512]{2,1,0:T(8,128)(2,1)S(1)}, u32[]{:S(2)}, u32[]{:S(2)}) collective-permute-start(bf16[32,32,512]{2,1,0:T(8,128)(2,1)S(1)} %bitcast.9), channel_id=1, source_target_pairs={{1,0},{2,1},{3,2},{5,4},{6,5},{7,6},{9,8},{10,9},{11,10},{13,12},{... | collective-permute-start | bytes 3145736 | tf_op jit(solution)/shard_map/ppermute | solution.py:186
  17.2 3.4 %collective-permute-start = (bf16[2,64,1536]{2,1,0:T(8,128)(2,1)}, bf16[2,64,1536]{2,1,0:T(8,128)(2,1)S(1)}, u32[]{:S(2)}, u32[]{:S(2)}) collective-permute-start(bf16[2,64,1536]{2,1,0:T(8,128)(2,1)} %slice.36), channel_id=1, source_target_pairs={{0,1},{4,5},{8,9},{12,13},{16,17},{20,21},{24,25},{28,29}} | collective-permute-start | bytes 1179656 | tf_op jit(solution)/shard_map/ppermute | solution.py:160
  17.9 19.0 %collective-permute-start.1 = (bf16[2,64,1536]{2,1,0:T(8,128)(2,1)}, bf16[2,64,1536]{2,1,0:T(8,128)(2,1)}, u32[]{:S(2)}, u32[]{:S(2)}) collective-permute-start(bf16[2,64,1536]{2,1,0:T(8,128)(2,1)} %slice.36), channel_id=1, source_target_pairs={{0,2},{4,6},{8,10},{12,14},{16,18},{20,22},{24,26},{28,30}} | collective-permute-start | bytes 1179656 | tf_op jit(solution)/shard_map/ppermute | solution.py:160
  19.2 17.7 %collective-permute-start.2 = (bf16[2,64,1536]{2,1,0:T(8,128)(2,1)}, bf16[2,64,1536]{2,1,0:T(8,128)(2,1)}, u32[]{:S(2)}, u32[]{:S(2)}) collective-permute-start(bf16[2,64,1536]{2,1,0:T(8,128)(2,1)} %slice.36), channel_id=1, source_target_pairs={{0,3},{4,7},{8,11},{12,15},{16,19},{20,23},{24,27},{28,31}} | collective-permute-start | bytes 1179656 | tf_op jit(solution)/shard_map/ppermute | solution.py:160
  20.6 24.3 %copy-start.12 = (bf16[2,64,1536]{2,1,0:T(8,128)(2,1)}, bf16[2,64,1536]{2,1,0:T(8,128)(2,1)S(1)}, u32[]{:S(2)}) copy-start(bf16[2,64,1536]{2,1,0:T(8,128)(2,1)S(1)} %collective-permute-done.refs_1_) | copy-start | bytes 1179652
  44.2 1.0 copy-start.11
  44.2 1.4 copy-start
  47.7 28.0 %collective-permute-start.5 = (bf16[32,32,512]{2,1,0:T(8,128)(2,1)S(1)}, bf16[32,32,512]{2,1,0:T(8,128)(2,1)S(1)}, u32[]{:S(2)}, u32[]{:S(2)}) collective-permute-start(bf16[32,32,512]{2,1,0:T(8,128)(2,1)S(1)} %bitcast.10), channel_id=1, source_target_pairs={{0,1},{1,2},{4,5},{5,6},{8,9},{9,10},{12,13},{13,14},{16,17},{17,1... | collective-permute-start | bytes 3145736 | tf_op jit(solution)/shard_map/ppermute | solution.py:193
  49.0 1.0 copy-start.4
  51.7 49.9 %copy-start.6 = (bf16[32,32,512]{2,0,1:T(8,128)(2,1)}, bf16[32,32,512]{2,0,1:T(8,128)(2,1)S(1)}, u32[]{:S(2)}) copy-start(bf16[32,32,512]{2,0,1:T(8,128)(2,1)S(1)} %copy.39) | copy-start | bytes 3145732
  51.7 46.5 %collective-permute-start.6 = (bf16[32,32,512]{2,1,0:T(8,128)(2,1)S(1)}, bf16[32,32,512]{2,1,0:T(8,128)(2,1)}, u32[]{:S(2)}, u32[]{:S(2)}) collective-permute-start(bf16[32,32,512]{2,1,0:T(8,128)(2,1)S(1)} %bitcast.12), channel_id=1, source_target_pairs={{0,1},{1,2},{2,3},{4,5},{5,6},{6,7},{8,9},{9,10},{10,11},{12,13},{... | collective-permute-start | bytes 3145736 | tf_op jit(solution)/shard_map/ppermute | solution.py:173
  55.6 42.7 %collective-permute-start.7 = (bf16[32,32,512]{2,1,0:T(8,128)(2,1)S(1)}, bf16[32,32,512]{2,1,0:T(8,128)(2,1)}, u32[]{:S(2)}, u32[]{:S(2)}) collective-permute-start(bf16[32,32,512]{2,1,0:T(8,128)(2,1)S(1)} %bitcast.13), channel_id=1, source_target_pairs={{1,0},{2,1},{3,2},{5,4},{6,5},{7,6},{9,8},{10,9},{11,10},{13,12},{... | collective-permute-start | bytes 3145736 | tf_op jit(solution)/shard_map/ppermute | solution.py:173
  76.7 53.9 %collective-permute-start.8 = (bf16[32,32,512]{2,1,0:T(8,128)(2,1)}, bf16[32,32,512]{2,1,0:T(8,128)(2,1)S(1)}, u32[]{:S(2)}, u32[]{:S(2)}) collective-permute-start(bf16[32,32,512]{2,1,0:T(8,128)(2,1)} %get-tuple-element.50.refs_1_), channel_id=1, source_target_pairs={{1,2},{2,3},{5,6},{6,7},{9,10},{10,11},{13,14},{14,15},{17,18},{18... | collective-permute-start | bytes 3145736 | tf_op jit(solution)/shard_map/ppermute | solution.py:173
  78.7 52.0 %collective-permute-start.9 = (bf16[32,32,512]{2,1,0:T(8,128)(2,1)}, bf16[32,32,512]{2,1,0:T(8,128)(2,1)}, u32[]{:S(2)}, u32[]{:S(2)}) collective-permute-start(bf16[32,32,512]{2,1,0:T(8,128)(2,1)} %get-tuple-element.51.refs_2_), channel_id=1, source_target_pairs={{1,0},{2,1},{5,4},{6,5},{9,8},{10,9},{13,12},{14,13},{17,16},{18,1... | collective-permute-start | bytes 3145736 | tf_op jit(solution)/shard_map/ppermute | solution.py:173
  98.2 0.7 copy-start.8
  101.7 56.1 %collective-permute-start.12 = (bf16[32,32,512]{2,1,0:T(8,128)(2,1)}, bf16[32,32,512]{2,1,0:T(8,128)(2,1)S(1)}, u32[]{:S(2)}, u32[]{:S(2)}) collective-permute-start(bf16[32,32,512]{2,1,0:T(8,128)(2,1)} %get-tuple-element.57.refs_1_), channel_id=1, source_target_pairs={{1,2},{2,3},{5,6},{6,7},{9,10},{10,11},{13,14},{14,15},{17,18},{18... | collective-permute-start | bytes 3145736 | tf_op jit(solution)/shard_map/ppermute | solution.py:173
  103.6 54.1 %collective-permute-start.13 = (bf16[32,32,512]{2,1,0:T(8,128)(2,1)}, bf16[32,32,512]{2,1,0:T(8,128)(2,1)S(1)}, u32[]{:S(2)}, u32[]{:S(2)}) collective-permute-start(bf16[32,32,512]{2,1,0:T(8,128)(2,1)} %get-tuple-element.58.refs_2_), channel_id=1, source_target_pairs={{1,0},{2,1},{5,4},{6,5},{9,8},{10,9},{13,12},{14,13},{17,16},{18,1... | collective-permute-start | bytes 3145736 | tf_op jit(solution)/shard_map/ppermute | solution.py:173
  142.1 15.6 %copy-start.3 = (bf16[32,32,512]{2,1,0:T(8,128)(2,1)}, bf16[32,32,512]{2,1,0:T(8,128)(2,1)S(1)}, u32[]{:S(2)}) copy-start(bf16[32,32,512]{2,1,0:T(8,128)(2,1)S(1)} %get-tuple-element.52.refs_3_) | copy-start | bytes 3145732
  142.1 38.4 %collective-permute-start.10 = (bf16[32,32,512]{2,1,0:T(8,128)(2,1)S(1)}, bf16[32,32,512]{2,1,0:T(8,128)(2,1)}, u32[]{:S(2)}, u32[]{:S(2)}) collective-permute-start(bf16[32,32,512]{2,1,0:T(8,128)(2,1)S(1)} %get-tuple-element.52.refs_3_), channel_id=1, source_target_pairs={{2,3},{6,7},{10,11},{14,15},{18,19},{22,23},{26,27},{30,31}} | collective-permute-start | bytes 3145736 | tf_op jit(solution)/shard_map/ppermute | solution.py:173
  144.4 36.1 %collective-permute-start.11 = (bf16[32,32,512]{2,1,0:T(8,128)(2,1)}, bf16[32,32,512]{2,1,0:T(8,128)(2,1)}, u32[]{:S(2)}, u32[]{:S(2)}) collective-permute-start(bf16[32,32,512]{2,1,0:T(8,128)(2,1)} %get-tuple-element.53.refs_4_), channel_id=1, source_target_pairs={{1,0},{5,4},{9,8},{13,12},{17,16},{21,20},{25,24},{29,28}} | collective-permute-start | bytes 3145736 | tf_op jit(solution)/shard_map/ppermute | solution.py:173
  146.1 11.7 %copy-start.1 = (bf16[32,32,512]{2,1,0:T(8,128)(2,1)S(1)}, bf16[32,32,512]{2,1,0:T(8,128)(2,1)}, u32[]{:S(2)}) copy-start(bf16[32,32,512]{2,1,0:T(8,128)(2,1)} %get-tuple-element.51.refs_2_) | copy-start | bytes 3145732
  146.1 11.7 %copy-start.2 = (bf16[32,32,512]{2,1,0:T(8,128)(2,1)S(1)}, bf16[32,32,512]{2,1,0:T(8,128)(2,1)}, u32[]{:S(2)}) copy-start(bf16[32,32,512]{2,1,0:T(8,128)(2,1)} %get-tuple-element.50.refs_1_) | copy-start | bytes 3145732
  146.1 11.7 %copy-start.5 = (bf16[32,32,512]{2,0,1:T(8,128)(2,1)S(1)}, bf16[32,32,512]{2,0,1:T(8,128)(2,1)}, u32[]{:S(2)}) copy-start(bf16[32,32,512]{2,0,1:T(8,128)(2,1)} %copy-done.4) | copy-start | bytes 3145732
  165.9 0.6 copy-start.9
  166.5 21.9 %collective-permute-start.14 = (bf16[32,32,512]{2,1,0:T(8,128)(2,1)S(1)}, bf16[32,32,512]{2,1,0:T(8,128)(2,1)}, u32[]{:S(2)}, u32[]{:S(2)}) collective-permute-start(bf16[32,32,512]{2,1,0:T(8,128)(2,1)S(1)} %get-tuple-element.60.refs_3_), channel_id=1, source_target_pairs={{2,3},{6,7},{10,11},{14,15},{18,19},{22,23},{26,27},{30,31}} | collective-permute-start | bytes 3145736 | tf_op jit(solution)/shard_map/ppermute | solution.py:173
  168.8 19.7 %collective-permute-start.15 = (bf16[32,32,512]{2,1,0:T(8,128)(2,1)S(1)}, bf16[32,32,512]{2,1,0:T(8,128)(2,1)}, u32[]{:S(2)}, u32[]{:S(2)}) collective-permute-start(bf16[32,32,512]{2,1,0:T(8,128)(2,1)S(1)} %get-tuple-element.61.refs_4_), channel_id=1, source_target_pairs={{1,0},{5,4},{9,8},{13,12},{17,16},{21,20},{25,24},{29,28}} | collective-permute-start | bytes 3145736 | tf_op jit(solution)/shard_map/ppermute | solution.py:173
  170.5 1.2 copy-start.7
  171.7 0.7 copy-start.10
Sparse Core Ops, SparseCore 0:
  47.8 34.2 all-gather.1
